TPU v7x, 32 devices: a whole 2x2x4 slice. The times are simulated.
32 devices in a mesh: req: 8 (over z, x), head: 2 (over y), side: 2 (over core).
Axes of the slice: x: 2, y: 2, z: 4, core: 2. Of those that a mesh axis runs over, the one named last changes fastest.
Arguments:
- query: bfloat16 [64, 128, 128], P(('req', 'side'), 'head'), may hold values from -40 to 40
- keys: bfloat16 [64, 8, 192, 128], P(('req', 'side'), 'head'), may hold values from -40 to 40
- values: bfloat16 [64, 8, 192, 128], P(('req', 'side'), 'head'), may hold values from -12 to 12
- lengths: int32 [64], P(('req', 'side')), may hold values from 2 to 192, as said below
- residual: bfloat16 [64, 16384], P(None, ('req', 'side')), may hold values from -6 to 6
- out_weight: bfloat16 [16384, 16384], P('head', ('req', 'side')), may hold values from -0.046875 to 0.046875
- norm_gain: float32 [16384], P(('req', 'side')), may hold values from 0.5 to 1.5
- gate_weight: bfloat16 [16384, 26624], P(('req', 'side'), 'head'), may hold values from -0.046875 to 0.046875
- up_weight: bfloat16 [16384, 26624], P(('req', 'side'), 'head'), may hold values from -0.046875 to 0.046875
- down_weight: bfloat16 [26624, 16384], P('head', ('req', 'side')), may hold values from -0.0390625 to 0.0390625
Outputs:
- output: bfloat16 [64, 16384], P('head', ('req', 'side'))
Inputs may be any that keep to these rules, and one draw needn't show every extreme that they name: `lengths`: the first request of each block of 4 requests has length 192.
All inputs are finite; a program needn't handle non-finite values.
Results may differ from a plain program's by a relative error of at most 0.0048.
Values may be sent and summed in bfloat16 or wider, within the bound.
A program may use at most 192 MiB of HBM per device.

v0:
```python
import math

import jax
import jax.numpy as jnp
from jax import lax
from jax.sharding import PartitionSpec as P

D = 16384


def shards(
    query,
    keys,
    values,
    lengths,
    residual,
    out_weight,
    norm_gain,
    gate_weight,
    up_weight,
    down_weight,
):
    local_reqs, local_heads, head_dim = query.shape
    local_kv = keys.shape[1]
    cache_len = keys.shape[2]
    group_size = local_heads // local_kv
    grouped = query.reshape(local_reqs, local_kv, group_size, head_dim)
    scores = jnp.einsum(
        "rkgd,rkpd->rkgp", grouped, keys, preferred_element_type=jnp.float32
    ) / math.sqrt(head_dim)
    positions = jnp.arange(cache_len, dtype=jnp.int32)
    usable = positions[None, :] < lengths[:, None]
    scores = jnp.where(usable[:, None, None, :], scores, -1e30)
    row_max = jnp.max(scores, axis=-1, keepdims=True)
    weights = jnp.exp(scores - row_max)
    weight_sum = jnp.sum(weights, axis=-1, keepdims=True)
    context = jnp.einsum(
        "rkgp,rkpd->rkgd", weights.astype(jnp.bfloat16), values, preferred_element_type=jnp.float32
    )
    attended = (
        (context / weight_sum).reshape(local_reqs, local_heads * head_dim).astype(jnp.bfloat16)
    )
    head_part = jnp.dot(
        lax.all_gather(attended, ("req", "side"), axis=0, tiled=True),
        out_weight,
        preferred_element_type=jnp.float32,
    )
    projected = lax.psum(head_part, "head")
    stream = residual.astype(jnp.float32) + projected
    squares = lax.psum(jnp.sum(stream * stream, axis=1), ("req", "side"))
    scaled = (stream * lax.rsqrt(squares[:, None] / D + 1e-05) * norm_gain).astype(jnp.bfloat16)
    gate_sum, up_sum = lax.psum(
        (
            jnp.dot(scaled, gate_weight, preferred_element_type=jnp.float32),
            jnp.dot(scaled, up_weight, preferred_element_type=jnp.float32),
        ),
        ("req", "side"),
    )
    hidden = (jax.nn.silu(gate_sum) * up_sum).astype(jnp.bfloat16)
    lowered = jnp.dot(hidden, down_weight, preferred_element_type=jnp.float32)
    reduced = lax.psum_scatter(lowered, "head", scatter_dimension=0, tiled=True)
    row_count = reduced.shape[0]
    own_rows = lax.dynamic_slice_in_dim(stream, lax.axis_index("head") * row_count, row_count, 0)
    return (own_rows + reduced).astype(jnp.bfloat16)


def solution(mesh):
    in_specs = (
        P(("req", "side"), "head", None),
        P(("req", "side"), "head", None, None),
        P(("req", "side"), "head", None, None),
        P(("req", "side")),
        P(None, ("req", "side")),
        P("head", ("req", "side")),
        P(("req", "side")),
        P(("req", "side"), "head"),
        P(("req", "side"), "head"),
        P("head", ("req", "side")),
    )
    out_specs = P("head", ("req", "side"))
    return jax.shard_map(shards, mesh=mesh, in_specs=in_specs, out_specs=out_specs, check_vma=False)
```

profile of v0, /device:TPU:0, one launch (start us, length us, event | category | flops | bytes accessed | tf_op | source)
XLA Modules:
  0.0 325.9 jit_solution(12499904257980625369)
XLA Ops:
  6.5 0.0 copy-start
  6.5 0.0 all-gather.3.cloned.1.call-start
  6.5 0.8 iota_compare_fusion
  7.3 0.3 copy-done
  7.7 1.4 fusion.11
  9.1 0.2 fusion.4
  9.4 1.5 fusion.3
  10.9 0.7 reshape.30
  11.5 0.0 all-gather.3.cloned.1.call-update
  11.6 0.0 all-reduce.4.cloned.1.call-start
  11.6 40.7 %all-gather.3.cloned.1.call-done = bf16[16,4,8192]{2,1,0:T(4,128)(2,1)} async-done(((bf16[1,4,8192]{2,1,0:T(4,128)(2,1)}), bf16[16,4,8192]{2,1,0:T(4,128)(2,1)}) %all-gather.3.cloned.1.call-update) | async-done | bytes 1048592 | tf_op jit(solution)/shard_map/all_gather | solution.py:44
  52.3 1.3 reshape.31
  53.7 0.0 copy-start.3
  53.7 0.0 copy-start.2
  53.7 9.5 %fusion.12 = f32[64,1024]{1,0:T(8,128)} fusion(bf16[64,8192]{1,0:T(8,128)(2,1)S(1)} %reshape.31, bf16[8192,1024]{1,0:T(8,128)(2,1)} %param.15), kind=kOutput, calls=%fused_computation.21 | convolution fusion | flops 1073741824 | bytes 18087936 | tf_op jit(solution)/shard_map/dot_general | solution.py:43
  63.2 0.0 all-reduce.4.cloned.1.call-update
  63.3 0.0 all-reduce.6.cloned.1.call-start
  63.3 22.2 %all-reduce.4.cloned.1.call-done = f32[64,1024]{1,0:T(8,128)} async-done(((f32[64,1024]{1,0:T(8,128)}), f32[64,1024]{1,0:T(8,128)}) %all-reduce.4.cloned.1.call-update) | async-done | bytes 262160 | tf_op jit(solution)/shard_map/psum | solution.py:48
  85.5 0.0 copy-done.3
  85.5 1.1 multiply_reduce_fusion
  86.6 32.7 %psum.29 = f32[64]{0:T(128)S(1)} all-reduce(f32[64]{0:T(128)S(1)} %get-tuple-element.7), channel_id=1, replica_groups=mesh['req'=8,'head'=2,'side'=2] {'req','side'}, use_global_device_ids=true, to_apply=%region_4.5 | all-reduce | flops 64 | bytes 512 | tf_op jit(solution)/shard_map/psum | solution.py:50
  119.3 0.0 copy-done.2
  119.3 13.1 %fusion.10 = f32[64,13312]{1,0:T(8,128)} fusion(bf16[1024,13312]{1,0:T(8,128)(2,1)} %param.17, f32[64,1024]{1,0:T(8,128)S(1)} %get-tuple-element.8, f32[1024]{0:T(1024)S(1)} %copy-done.2, f32[64]{0:T(128)S(1)} %add_rsqrt_fusion), kind=kOutput, calls=%fused_computation.19 | convolution fusion | flops 1745027072 | bytes 30937344 | tf_op jit(solution)/shard_map/dot_general | solution.py:54
  132.5 13.1 %fusion.9 = f32[64,13312]{1,0:T(8,128)} fusion(bf16[1024,13312]{1,0:T(8,128)(2,1)} %param.18, f32[64,1024]{1,0:T(8,128)S(1)} %get-tuple-element.8, f32[1024]{0:T(1024)S(1)} %copy-done.2, f32[64]{0:T(128)S(1)} %add_rsqrt_fusion), kind=kOutput, calls=%fused_computation.18 | convolution fusion | flops 1745027072 | bytes 30937344 | tf_op jit(solution)/shard_map/dot_general | solution.py:55
  145.6 0.0 all-reduce.6.cloned.1.call-update
  145.6 0.0 reduce-scatter.2.cloned.1.call-start
  145.6 144.1 %all-reduce.6.cloned.1.call-done = (f32[64,13312]{1,0:T(8,128)}, f32[64,13312]{1,0:T(8,128)}) async-done(((f32[64,13312]{1,0:T(8,128)}, f32[64,13312]{1,0:T(8,128)}), (f32[64,13312]{1,0:T(8,128)}, f32[64,13312]{1,0:T(8,128)})) %all-reduce.6.cloned.1.call-update) | async-done | bytes 6815760 | tf_op jit(solution)/shard_map/psum | solution.py:52
  289.8 16.4 %fusion = f32[64,1024]{1,0:T(8,128)} fusion(bf16[13312,1024]{1,0:T(8,128)(2,1)} %param.19, f32[64,13312]{1,0:T(8,128)} %get-tuple-element.5, f32[64,13312]{1,0:T(8,128)} %get-tuple-element.6), kind=kOutput, calls=%fused_computation.1 | convolution fusion | flops 1749942272 | bytes 34340864 | tf_op jit(solution)/shard_map/dot_general | solution.py:60
  306.2 0.0 reduce-scatter.2.cloned.1.call-update
  306.2 11.6 %reduce-scatter.2.cloned.1.call-done = f32[32,1024]{1,0:T(8,128)} async-done(((f32[64,1024]{1,0:T(8,128)}), f32[32,1024]{1,0:T(8,128)}) %reduce-scatter.2.cloned.1.call-update) | async-done | bytes 131088 | tf_op jit(solution)/shard_map/reduce_scatter | solution.py:61
  317.9 1.5 add_convert_fusion
  319.4 0.0 copy-done.1
  (2 shorter events, 0.0 us)
Async XLA Ops:
  6.5 1.1 copy-start
  6.5 45.8 %all-gather.3.cloned.1.call-start = ((), (), s32[]{:S(2)}) async-start(), calls=%async_computation.3 | async-start | bytes 1114112 | tf_op jit(solution)/shard_map/all_gather | solution.py:44
  11.6 74.0 %all-reduce.4.cloned.1.call-start = ((), (), s32[]{:S(2)}) async-start(), calls=%async_computation.1 | async-start | bytes 524288 | tf_op jit(solution)/shard_map/psum | solution.py:48
  53.7 31.8 %copy-start.3 = (bf16[64,1024]{1,0:T(8,128)(2,1)S(1)}, bf16[64,1024]{1,0:T(8,128)(2,1)}, u32[]{:S(2)}) copy-start(bf16[64,1024]{1,0:T(8,128)(2,1)} %param.14) | copy-start | bytes 393220
  53.7 65.6 %copy-start.2 = (f32[1024]{0:T(1024)S(1)}, f32[1024]{0:T(1024)}, u32[]{:S(2)}) copy-start(f32[1024]{0:T(1024)} %param.16) | copy-start | bytes 12292
  63.3 226.5 %all-reduce.6.cloned.1.call-start = ((), (), s32[]{:S(2)}) async-start(), calls=%async_computation.4 | async-start | bytes 13631488 | tf_op jit(solution)/shard_map/psum | solution.py:52
  145.6 172.3 %reduce-scatter.2.cloned.1.call-start = ((), (), s32[]{:S(2)}) async-start(), calls=%async_computation.2 | async-start | bytes 393216 | tf_op jit(solution)/shard_map/reduce_scatter | solution.py:61
  289.8 29.6 %copy-start.1 = (bf16[4,4,192,128]{3,2,1,0:T(8,128)(2,1)S(1)}, bf16[4,4,192,128]{3,2,1,0:T(8,128)(2,1)}, u32[]{:S(2)}) copy-start(bf16[4,4,192,128]{3,2,1,0:T(8,128)(2,1)} %param.11) | copy-start | bytes 2359300
Sparse Core Ops, SparseCore 0:
  11.7 40.6 all-gather.2
  63.4 22.1 all-reduce.3
  145.7 144.0 all-reduce.5
  306.3 11.4 reduce-scatter.1
where the time goes:
time: 326 us
  waiting for transfers between devices  219 us (67%)
  matrix products  55.1 us (17%)
  blocking collectives  32.7 us (10%)
  between operations  13.2 us (4%)
  other arithmetic  3.68 us (1%)
    psum x1, waiting for transfers between devices, shards(): lax.psum((jnp.dot(scaled, gate_weight, preferred_element_type=jnp.float32...  144 us
    all_gather x1, waiting for transfers between devices, shards(): lax.all_gather(attended, ('req', 'side'), axis=0, tiled=True)  40.7 us
    psum x1, blocking collectives, shards(): squares = lax.psum(jnp.sum(stream * stream, axis=1), ('req', 'side'))  32.7 us
    psum x1, waiting for transfers between devices, shards(): projected = lax.psum(head_part, 'head')  22.2 us
    dot_general x1, matrix products, shards(): lowered = jnp.dot(hidden, down_weight, preferred_element_type=jnp.float32)  16.4 us
    dot_general x1, matrix products, shards(): jnp.dot(scaled, gate_weight, preferred_element_type=jnp.float32)  13.1 us
    dot_general x1, matrix products, shards(): jnp.dot(scaled, up_weight, preferred_element_type=jnp.float32)  13.1 us
    reduce_scatter x1, waiting for transfers between devices, shards(): reduced = lax.psum_scatter(lowered, 'head', scatter_dimension=0, tiled=True)  11.6 us
  transfers between devices with their start and end apart: 4, of which 4 were waited for; matrix products, arithmetic and copies ran while one was open for 0% of the time, Pallas kernels for 0%

commit v1 on v0

v1 whole, which is shorter than its diff:
```python
import functools
import math

import jax
import jax.numpy as jnp
from jax import lax
from jax.experimental import pallas as pl
from jax.experimental.pallas import tpu as pltpu
from jax.sharding import PartitionSpec as P

MESH = pl.DeviceIdType.MESH
F32 = jnp.float32
BF16 = jnp.bfloat16


def low_bit(k):
    return (k & -k).bit_length() - 1


def flip(index, k):
    out = index
    b = 0
    while (1 << b) <= k:
        if k & (1 << b):
            bit = lax.rem(lax.div(index, jnp.int32(1 << b)), jnp.int32(2))
            out = out + (1 - 2 * bit) * (1 << b)
        b += 1
    return out


def tiles(width, step):
    return [(s, min(step, width - s)) for s in range(0, width, step)]


def layer_kernel(
    n_req, quarters, d_model,
    att_ref, res_ref, gain_ref, ow_hbm, gate_hbm, up_hbm, down_hbm,
    out_ref,
    ow, down2, gu, ag, xq, stream, xs, psend, precv, sqsend, sqrecv,
    acc, s_send, s_recv, t_send, t_recv, hid, low, low_send, low_recv,
    ow_sem, gu_sem, down_sem,
    ag_ss, ag_rs, agc_ss, agc_rs,
    p_ss, p_rs, sq_ss, sq_rs,
    sc_ss, sc_rs, t_ss, t_rs,
    h_ss, h_rs, hc_ss, hc_rs, l_ss, l_rs,
):
    bits = n_req.bit_length() - 1
    me = lax.axis_index("req")
    head = lax.axis_index("head")
    side = lax.axis_index("side")
    rows, width = stream.shape
    half = rows // 2
    chunk = acc.shape[-1]
    k_part = xq.shape[-1]
    in_ow = ow.shape[0] // chunk
    gu_slots = gu.shape[0]

    def req_peer(b):
        return (flip(me, 1 << b), head, side)

    sibling = (me, head, 1 - side)
    across = (me, 1 - head, side)

    def ow_copy(q):
        part = pl.ds(q * k_part, k_part)
        return pltpu.make_async_copy(ow_hbm.at[part], ow.at[part], ow_sem.at[q])

    def gu_copies(k):
        columns = pl.ds(pl.multiple_of(flip(me, k) * chunk, 128), chunk)
        slot = (n_req - 1 - k) % gu_slots
        return [
            pltpu.make_async_copy(hbm.at[:, columns], gu.at[slot, j], gu_sem.at[slot, j])
            for j, hbm in enumerate((gate_hbm, up_hbm))
        ]

    def down_place(k):
        if k < in_ow:
            return ow.at[pl.ds(k * chunk, chunk)]
        return down2.at[k - in_ow]

    def down_copy(k):
        part = pl.ds(pl.multiple_of(flip(me, k) * chunk, 128), chunk)
        return pltpu.make_async_copy(down_hbm.at[part], down_place(k), down_sem.at[k])

    for q in range(quarters):
        ow_copy(q).start()
    for k in range(n_req - 1, n_req - 1 - gu_slots, -1):
        for c in gu_copies(k):
            c.start()
    for k in range(in_ow, n_req):
        down_copy(k).start()

    barrier = pltpu.get_barrier_semaphore()
    peers = [sibling, across] + [req_peer(b) for b in range(bits)]
    for peer in peers:
        pl.semaphore_signal(barrier, inc=1, device_id=peer, device_id_type=MESH)
    pl.semaphore_wait(barrier, len(peers))

    def remote(src, dst, ss, rs, peer):
        return pltpu.make_async_remote_copy(
            src_ref=src, dst_ref=dst, send_sem=ss, recv_sem=rs, device_id=peer, device_id_type=MESH
        )

    def ag_tree(m):
        b = low_bit(m)
        block = ag.at[flip(me, m ^ (1 << b)), side]
        return remote(block, block, ag_ss.at[m], ag_rs.at[m], req_peer(b))

    def ag_tree_arrival(m):
        block = ag.at[flip(me, m), side]
        return remote(block, block, ag_ss.at[m], ag_rs.at[m], req_peer(low_bit(m)))

    def ag_core(k):
        block = ag.at[flip(me, k), side]
        return remote(block, block, agc_ss.at[k], agc_rs.at[k], sibling)

    def ag_core_arrival(k):
        block = ag.at[flip(me, k), 1 - side]
        return remote(block, block, agc_ss.at[k], agc_rs.at[k], sibling)

    def hid_tree(m):
        b = low_bit(m)
        return remote(
            hid.at[m ^ (1 << b), 0], hid.at[m, 0], h_ss.at[m], h_rs.at[m], req_peer(b)
        )

    def hid_core(k):
        return remote(hid.at[k, 0], hid.at[k, 1], hc_ss.at[k], hc_rs.at[k], sibling)

    def forward(k, tree, core):
        top = bits if k == 0 else low_bit(k)
        for b in range(top - 1, -1, -1):
            tree(k | (1 << b)).start()
        core(k).start()

    arrival = sorted(range(1, n_req), key=lambda k: (bin(k).count("1"), -low_bit(k)))

    ag[me, side] = att_ref[...]
    forward(0, ag_tree, ag_core)
    for k in arrival:
        ag_tree_arrival(k).wait_recv()
        forward(k, ag_tree, ag_core)
    for k in range(n_req):
        ag_core_arrival(k).wait_recv()

    local = rows // (2 * n_req)
    per = ag.shape[2]
    total_rows = 2 * n_req * per
    request = lax.broadcasted_iota(jnp.int32, (rows, total_rows), 0)
    held = lax.broadcasted_iota(jnp.int32, (rows, total_rows), 1)
    for q in range(quarters):
        wanted = (request // local) * per + q * local + request % local
        pick = jnp.where(held == wanted, 1.0, 0.0).astype(BF16)
        for s, w in tiles(k_part, 512):
            gathered = ag[:, :, :, s : s + w].reshape(total_rows, w)
            xq[q, :, s : s + w] = jnp.dot(pick, gathered, preferred_element_type=F32).astype(BF16)

    halves = psend.shape[0]
    wide = width // halves

    def p_copy(n):
        return remote(psend.at[n], precv.at[n], p_ss.at[n], p_rs.at[n], across)

    for n in range(halves):
        cols = slice(n * wide, (n + 1) * wide)
        total = None
        for q in range(quarters):
            if n == 0:
                ow_copy(q).wait()
            part = jnp.dot(
                xq[q], ow[q * k_part : (q + 1) * k_part, cols], preferred_element_type=F32
            )
            total = part if total is None else total + part
        psend[n] = total.astype(BF16)
        p_copy(n).start()
        stream[:, cols] = total + res_ref[:, cols].astype(F32)
    for n in range(halves):
        cols = slice(n * wide, (n + 1) * wide)
        p_copy(n).wait_recv()
        stream[:, cols] = stream[:, cols] + precv[n].astype(F32)

    own = pl.ds(pl.multiple_of(side * half, half), half)
    other = pl.ds(pl.multiple_of((1 - side) * half, half), half)
    xs[0:half, :] = (stream[own, :] * gain_ref[...]).astype(BF16)
    xs[half:rows, :] = (stream[other, :] * gain_ref[...]).astype(BF16)
    value = stream[...]
    sqsend[0] = jnp.broadcast_to(jnp.sum(value * value, axis=1, keepdims=True), (rows, 128))

    def sq_copy(b):
        peer = sibling if b == 0 else req_peer(b - 1)
        return remote(sqsend.at[b], sqrecv.at[b], sq_ss.at[b], sq_rs.at[b], peer)

    sq_copy(0).start()

    def sq_step(b):
        sq_copy(b).wait_recv()
        sqsend[b + 1] = sqsend[b] + sqrecv[b]
        if b < bits:
            sq_copy(b + 1).start()

    def core_copy(k):
        return remote(s_send.at[k], s_recv.at[k], sc_ss.at[k], sc_rs.at[k], sibling)

    def tree_copy(k):
        return remote(t_send.at[k], t_recv.at[k], t_ss.at[k], t_rs.at[k], req_peer(low_bit(k)))

    def compute(k):
        slot = (n_req - 1 - k) % gu_slots
        for j, c in enumerate(gu_copies(k)):
            c.wait()
            for s, w in tiles(chunk, 512):
                y = jnp.dot(xs[...], gu[slot, j, :, s : s + w], preferred_element_type=F32)
                acc[k, j, :, s : s + w] = y[0:half]
                s_send[k, j, :, s : s + w] = y[half:rows].astype(BF16)
        core_copy(k).start()
        if k - gu_slots >= 0:
            for c in gu_copies(k - gu_slots):
                c.start()

    def core_done(k):
        core_copy(k).wait_recv()
        if k % 2 == 1:
            t_send[k] = (acc[k] + s_recv[k].astype(F32)).astype(BF16)
            tree_copy(k).start()
        else:
            acc[k] = acc[k] + s_recv[k].astype(F32)

    def summed(k, j, s, w):
        out = acc[k, j, :, s : s + w]
        for b in range(bits if k == 0 else low_bit(k)):
            out = out + t_recv[k | (1 << b), j, :, s : s + w].astype(F32)
        return out

    def tree_wait(k):
        for b in range(bits if k == 0 else low_bit(k)):
            tree_copy(k | (1 << b)).wait_recv()

    def pass_on(k):
        tree_wait(k)
        for j in range(2):
            for s, w in tiles(chunk, 512):
                t_send[k, j, :, s : s + w] = summed(k, j, s, w).astype(BF16)
        tree_copy(k).start()

    for step, k in enumerate(range(n_req - 1, -1, -1)):
        compute(k)
        if step < in_ow and step < n_req:
            down_copy(step).start()
        if k + 1 < n_req:
            core_done(k + 1)
        late = k + 3
        if late < n_req and late % 2 == 0 and late > 0:
            pass_on(late)
        if step <= bits:
            sq_step(step)
    core_done(0)
    if n_req > 2:
        pass_on(2)
    tree_wait(0)

    scale = lax.rsqrt(sqsend[bits + 1, own, 0:1] / d_model + 1e-05)
    for s, w in tiles(chunk, 512):
        gate = summed(0, 0, s, w) * scale
        up = summed(0, 1, s, w) * scale
        hid[0, 0, :, s : s + w] = (gate / (1.0 + jnp.exp(-gate)) * up).astype(BF16)

    forward(0, hid_tree, hid_core)

    def lower(k, first):
        hid_core(k).wait_recv()
        down_copy(k).wait()
        place = down_place(k)
        x = hid[k].reshape(rows, chunk)
        for s, w in tiles(width, 512):
            y = jnp.dot(x, place[:, s : s + w], preferred_element_type=F32)
            if first:
                low[:, s : s + w] = y
            else:
                low[:, s : s + w] = low[:, s : s + w] + y

    pending = [0]
    for k in arrival:
        hid_tree(k).wait_recv()
        forward(k, hid_tree, hid_core)
        if len(pending) > 2 or k == arrival[0]:
            j = pending.pop(0)
            lower(j, j == 0)
        pending.append(k)
    for j in pending:
        lower(j, j == 0)

    mine = pl.ds(pl.multiple_of(lax.rem(head + side, 2) * half, half), half)
    theirs = pl.ds(pl.multiple_of(lax.rem(head + side + 1, 2) * half, half), half)
    low_send[...] = low[theirs, :]
    last = remote(low_send, low_recv, l_ss.at[0], l_rs.at[0], across)
    last.start()
    kept = stream[pl.ds(pl.multiple_of(head * half, half), half), :] + low[mine, :]
    last.wait_recv()
    out_ref[...] = (kept + low_recv[...]).astype(out_ref.dtype)

    last.wait_send()
    for n in range(halves):
        p_copy(n).wait_send()
    for b in range(bits + 1):
        sq_copy(b).wait_send()
    for k in range(n_req):
        ag_core(k).wait_send()
        core_copy(k).wait_send()
        hid_core(k).wait_send()
        if k > 0:
            ag_tree(k).wait_send()
            tree_copy(k).wait_send()
            hid_tree(k).wait_send()


def layer(att, residual, norm_gain, out_weight, gate_weight, up_weight, down_weight, n_req, d_model):
    rows, width = residual.shape
    per, k_part = att.shape
    k_local = out_weight.shape[0]
    quarters = k_local // k_part
    ff = gate_weight.shape[1]
    chunk = ff // n_req
    half = rows // 2
    bits = n_req.bit_length() - 1
    in_ow = min(n_req, -(-k_local // chunk))
    gu_slots = min(2, n_req)
    dma = lambda *shape: pltpu.SemaphoreType.DMA(shape)
    vmem = lambda shape, dtype: pltpu.VMEM(shape, dtype)
    piece = (n_req, 2, half, chunk)
    scratch = [
        vmem((max(in_ow * chunk, k_local), width), BF16),
        vmem((max(n_req - in_ow, 1), chunk, width), BF16),
        vmem((gu_slots, 2, width, chunk), BF16),
        vmem((n_req, 2, per, k_part), BF16),
        vmem((quarters, rows, k_part), BF16),
        vmem((rows, width), F32),
        vmem((rows, width), BF16),
        vmem((2, rows, width // 2), BF16),
        vmem((2, rows, width // 2), BF16),
        vmem((bits + 2, rows, 128), F32),
        vmem((bits + 1, rows, 128), F32),
        vmem(piece, F32),
        vmem(piece, BF16),
        vmem(piece, BF16),
        vmem(piece, BF16),
        vmem(piece, BF16),
        vmem(piece, BF16),
        vmem((rows, width), F32),
        vmem((half, width), F32),
        vmem((half, width), F32),
        dma(quarters), dma(gu_slots, 2), dma(n_req),
        dma(n_req), dma(n_req), dma(n_req), dma(n_req),
        dma(2), dma(2), dma(bits + 1), dma(bits + 1),
        dma(n_req), dma(n_req), dma(n_req), dma(n_req),
        dma(n_req), dma(n_req), dma(n_req), dma(n_req), dma(1), dma(1),
    ]
    in_vmem = pl.BlockSpec(memory_space=pltpu.VMEM)
    anywhere = pl.BlockSpec(memory_space=pl.ANY)
    weights = k_local * width + 2 * width * ff + ff * width
    return pl.pallas_call(
        functools.partial(layer_kernel, n_req, quarters, d_model),
        out_shape=jax.ShapeDtypeStruct((half, width), BF16),
        in_specs=[in_vmem] * 3 + [anywhere] * 4,
        out_specs=in_vmem,
        scratch_shapes=scratch,
        compiler_params=pltpu.CompilerParams(
            collective_id=0, has_side_effects=True, vmem_limit_bytes=60 * 1024 * 1024
        ),
        cost_estimate=pl.CostEstimate(
            flops=2 * rows * weights, bytes_accessed=2 * weights, transcendentals=0
        ),
    )(att, residual, norm_gain.reshape(1, width), out_weight, gate_weight, up_weight, down_weight)


def attention(query, keys, values, lengths):
    local_reqs, local_heads, head_dim = query.shape
    local_kv = keys.shape[1]
    cache_len = keys.shape[2]
    group_size = local_heads // local_kv
    grouped = query.reshape(local_reqs, local_kv, group_size, head_dim)
    scores = jnp.einsum(
        "rkgd,rkpd->rkgp", grouped, keys, preferred_element_type=F32
    ) / math.sqrt(head_dim)
    positions = jnp.arange(cache_len, dtype=jnp.int32)
    usable = positions[None, :] < lengths[:, None]
    scores = jnp.where(usable[:, None, None, :], scores, -1e30)
    row_max = jnp.max(scores, axis=-1, keepdims=True)
    weights = jnp.exp(scores - row_max)
    weight_sum = jnp.sum(weights, axis=-1, keepdims=True)
    context = jnp.einsum(
        "rkgp,rkpd->rkgd", weights.astype(BF16), values, preferred_element_type=F32
    )
    return (context / weight_sum).reshape(local_reqs, local_heads * head_dim).astype(BF16)


def plain_shards(
    d_model, query, keys, values, lengths, residual, out_weight, norm_gain, gate_weight, up_weight, down_weight
):
    attended = attention(query, keys, values, lengths)
    head_part = jnp.dot(
        lax.all_gather(attended, ("req", "side"), axis=0, tiled=True),
        out_weight,
        preferred_element_type=F32,
    )
    projected = lax.psum(head_part, "head")
    stream = residual.astype(F32) + projected
    squares = lax.psum(jnp.sum(stream * stream, axis=1), ("req", "side"))
    scaled = (stream * lax.rsqrt(squares[:, None] / d_model + 1e-05) * norm_gain).astype(BF16)
    gate_sum, up_sum = lax.psum(
        (
            jnp.dot(scaled, gate_weight, preferred_element_type=F32),
            jnp.dot(scaled, up_weight, preferred_element_type=F32),
        ),
        ("req", "side"),
    )
    hidden = (jax.nn.silu(gate_sum) * up_sum).astype(BF16)
    lowered = jnp.dot(hidden, down_weight, preferred_element_type=F32)
    reduced = lax.psum_scatter(lowered, "head", scatter_dimension=0, tiled=True)
    row_count = reduced.shape[0]
    own_rows = lax.dynamic_slice_in_dim(stream, lax.axis_index("head") * row_count, row_count, 0)
    return (own_rows + reduced).astype(BF16)


def fused_shards(
    n_req, d_model, query, keys, values, lengths, residual, out_weight, norm_gain, gate_weight, up_weight, down_weight
):
    attended = attention(query, keys, values, lengths)
    local_reqs, k_local = attended.shape
    quarters = 16 // local_reqs
    block = attended.reshape(local_reqs, quarters, k_local // quarters)
    block = block.transpose(1, 0, 2).reshape(16, k_local // quarters)
    return layer(block, residual, norm_gain, out_weight, gate_weight, up_weight, down_weight, n_req, d_model)


def solution(mesh):
    n_req, n_head, n_side = mesh.shape["req"], mesh.shape["head"], mesh.shape["side"]

    def shards(query, keys, values, lengths, residual, out_weight, norm_gain, gate_weight, up_weight, down_weight):
        rows, width = residual.shape
        local_reqs = query.shape[0]
        d_model = width * n_req * n_side
        ff = gate_weight.shape[1]
        fits = (
            n_side == 2
            and n_head == 2
            and n_req >= 4
            and n_req & (n_req - 1) == 0
            and ff % (n_req * 128) == 0
            and rows % 32 == 0
            and 16 % local_reqs == 0
            and out_weight.shape[0] % ((16 // local_reqs) * 128) == 0
        )
        body = functools.partial(fused_shards, n_req, d_model) if fits else functools.partial(plain_shards, d_model)
        return body(query, keys, values, lengths, residual, out_weight, norm_gain, gate_weight, up_weight, down_weight)

    in_specs = (
        P(("req", "side"), "head", None),
        P(("req", "side"), "head", None, None),
        P(("req", "side"), "head", None, None),
        P(("req", "side")),
        P(None, ("req", "side")),
        P("head", ("req", "side")),
        P(("req", "side")),
        P(("req", "side"), "head"),
        P(("req", "side"), "head"),
        P("head", ("req", "side")),
    )
    out_specs = P("head", ("req", "side"))
    return jax.shard_map(shards, mesh=mesh, in_specs=in_specs, out_specs=out_specs, check_vma=False)
```

time: 326 us -> 87.5 us (0.27)
  waiting for transfers between devices: 219 us -> 0 us
  Pallas kernels: 0 us -> 80.7 us
  matrix products: 55.1 us -> 2.94 us
  blocking collectives: 32.7 us -> 0 us
  between operations: 13.2 us -> 0.03 us
    psum x2 -> x0, waiting for transfers between devices: 166 us -> none  [the longest x1 144 us: shards(): lax.psum((jnp.dot(scaled, gate_weight, preferred_element_type=jnp.float32...]
    pallas_call x0 -> x1, Pallas kernels: none -> 80.7 us  [layer(): pl.pallas_call(functools.partial(layer_kernel, n_req, quarters, d_model),...]
    dot_general x6 -> x2, matrix products: 55.1 us -> 2.94 us  [the longest x1 1.51 us: attention(): jnp.einsum('rkgp,rkpd->rkgd', weights.astype(BF16), values, preferred_ele...]
    all_gather x1 -> x0, waiting for transfers between devices: 40.7 us -> none  [shards(): lax.all_gather(attended, ('req', 'side'), axis=0, tiled=True)]
    psum x1 -> x0, blocking collectives: 32.7 us -> none  [shards(): squares = lax.psum(jnp.sum(stream * stream, axis=1), ('req', 'side'))]
    reduce_scatter x1 -> x0, waiting for transfers between devices: 11.6 us -> none  [shards(): reduced = lax.psum_scatter(lowered, 'head', scatter_dimension=0, tiled=True)]
  transfers between devices with their start and end apart: 4 -> 0, of which waited for: 4 -> 0; matrix products, arithmetic and copies ran while one was open for 0% -> 0% of each run, Pallas kernels for 0% -> 0%
where the time goes in v1:
time: 87.5 us; the launch traced here: 87.2 us
  Pallas kernels  80.7 us (92%)
  matrix products  2.94 us (3%)
  local copies, waits for them, and re-layouts  2.56 us (3%)
  other arithmetic  1.03 us (1%)
    pallas_call x1, Pallas kernels, layer(): pl.pallas_call(functools.partial(layer_kernel, n_req, quarters, d_model),...  80.7 us
    unnamed x3, local copies, waits for them, and re-layouts  1.82 us

profile of v1, /device:TPU:0, one launch (start us, length us, event | category | flops | bytes accessed | tf_op | source)
XLA Modules:
  0.0 87.2 jit_solution(5238850885003821076)
XLA Ops:
  0.0 0.0 copy-start
  0.0 0.8 iota_compare_fusion
  0.8 0.3 copy-done
  1.2 1.4 %fusion.6 = (f32[4,4,16]{2,1,0:T(4,128)S(1)}, f32[4,4,16,192]{3,2,1,0:T(8,128)S(1)}) fusion(bf16[4,4,16,128]{3,2,1,0:T(8,128)(2,1)} %bitcast.11, bf16[4,4,192,128]{3,2,1,0:T(8,128)(2,1)S(1)} %copy-done, pred[4,192]{1,0:T(4,128)(4,1)S(1)} %iota_compare_fusion), kind=kOutput, calls=%fused_computation.10 | convolution fusion | flops 12730112 | bytes 1050368 | tf_op jit(solution)/shard_map/rkgd,rkpd->rkgp/dot_general | solution.py:381
  2.6 0.2 fusion.2
  2.8 1.5 %fusion.1 = bf16[4,4,16,128]{3,2,1,0:T(8,128)(2,1)S(1)} fusion(bf16[4,4,192,128]{3,2,1,0:T(8,128)(2,1)} %param.12, f32[4,4,16,192]{3,2,1,0:T(8,128)S(1)} %get-tuple-element.6, f32[4,4,16]{2,1,0:T(4,128)S(1)} %get-tuple-element.5, f32[4,4,16]{2,1,0:T(4,128)S(1)} %fusion.2), kind=kOutput, calls=%fused_computation.3 | convolution fusion | flops 12746752 | bytes 1050624 | tf_op jit(solution)/shard_map/rkgp,rkpd->rkgd/dot_general | solution.py:390
  4.4 0.1 copy.13
  4.4 0.6 reshape.33.att_ref
  5.1 80.7 %shard_map.100 = bf16[32,1024]{1,0:T(8,128)(2,1)} custom-call(bf16[16,2048]{1,0:T(8,128)(2,1)} %reshape.33.att_ref, bf16[64,1024]{1,0:T(8,128)(2,1)} %res_ref.1, f32[1,1024]{1,0:T(1,128)} %bitcast.12, bf16[8192,1024]{1,0:T(8,128)(2,1)} %ow_hbm.1, bf16[1024,13312]{1,0:T(8,128)(2,1)} %gate_hbm.1, bf16[1024,13312]{1,0:T(8,128)(2,1)} %up_hbm.1, ...), custom_call_target="tpu_custom_call" | custom-call | flops 6308233216 | bytes 98566144 | tf_op jit(solution)/shard_map/pallas_call | solution.py:360
  85.7 1.5 %copy.15 = bf16[32,1024]{1,0:T(8,128)(2,1)} copy(bf16[32,1024]{1,0:T(8,128)(2,1)} %shard_map.100) | data formatting | bytes 131072
  (1 shorter events, 0.0 us)
Async XLA Ops:
  0.0 1.1 %copy-start = (bf16[4,4,192,128]{3,2,1,0:T(8,128)(2,1)S(1)}, bf16[4,4,192,128]{3,2,1,0:T(8,128)(2,1)}, u32[]{:S(2)}) copy-start(bf16[4,4,192,128]{3,2,1,0:T(8,128)(2,1)} %param.11) | copy-start | bytes 2359300

commit v2 on v1

--- a/solution.py
+++ b/solution.py
@@ -34,9 +34,9 @@
 
 def layer_kernel(
     n_req, quarters, d_model,
-    att_ref, res_ref, gain_ref, ow_hbm, gate_hbm, up_hbm, down_hbm,
+    len_ref, query_ref, key_ref, value_ref, res_ref, gain_ref, ow_hbm, gate_hbm, up_hbm, down_hbm,
     out_ref,
-    ow, down2, gu, ag, xq, stream, xs, psend, precv, sqsend, sqrecv,
+    ctx, ow, down2, gu, ag, xq, stream, xs, psend, precv, sqsend, sqrecv,
     acc, s_send, s_recv, t_send, t_recv, hid, low, low_send, low_recv,
     ow_sem, gu_sem, down_sem,
     ag_ss, ag_rs, agc_ss, agc_rs,
@@ -94,6 +94,24 @@
     peers = [sibling, across] + [req_peer(b) for b in range(bits)]
     for peer in peers:
         pl.semaphore_signal(barrier, inc=1, device_id=peer, device_id_type=MESH)
+
+    local_reqs, local_kv, cache_len, head_dim = key_ref.shape
+    group = query_ref.shape[1] // local_kv
+    positions = lax.broadcasted_iota(jnp.int32, (group, cache_len), 1)
+    for g in range(local_kv):
+        for r in range(local_reqs):
+            scores = lax.dot_general(
+                query_ref[r, g * group : (g + 1) * group, :], key_ref[r, g],
+                (((1,), (1,)), ((), ())), preferred_element_type=F32,
+            ) / math.sqrt(head_dim)
+            scores = jnp.where(positions < len_ref[r], scores, -1e30)
+            weights = jnp.exp(scores - jnp.max(scores, axis=1, keepdims=True))
+            weight_sum = jnp.sum(weights, axis=1, keepdims=True)
+            context = jnp.dot(weights.astype(BF16), value_ref[r, g], preferred_element_type=F32)
+            ctx[g * local_reqs + r] = context / weight_sum
+    for h in range(group):
+        ag[me, side, :, h * head_dim : (h + 1) * head_dim] = ctx[:, h, :].astype(BF16)
+
     pl.semaphore_wait(barrier, len(peers))
 
     def remote(src, dst, ss, rs, peer):
@@ -133,9 +151,11 @@
             tree(k | (1 << b)).start()
         core(k).start()
 
-    arrival = sorted(range(1, n_req), key=lambda k: (bin(k).count("1"), -low_bit(k)))
-
-    ag[me, side] = att_ref[...]
+    arrival = sorted(
+        range(1, n_req),
+        key=lambda k: (bin(k).count("1"), low_bit(k) if k & (k - 1) == 0 else -low_bit(k)),
+    )
+
     forward(0, ag_tree, ag_core)
     for k in arrival:
         ag_tree_arrival(k).wait_recv()
@@ -211,7 +231,7 @@
             for s, w in tiles(chunk, 512):
                 y = jnp.dot(xs[...], gu[slot, j, :, s : s + w], preferred_element_type=F32)
                 acc[k, j, :, s : s + w] = y[0:half]
-                s_send[k, j, :, s : s + w] = y[half:rows].astype(BF16)
+                s_send[k, j, :, s : s + w] = y[half:rows]
         core_copy(k).start()
         if k - gu_slots >= 0:
             for c in gu_copies(k - gu_slots):
@@ -220,10 +240,10 @@
     def core_done(k):
         core_copy(k).wait_recv()
         if k % 2 == 1:
-            t_send[k] = (acc[k] + s_recv[k].astype(F32)).astype(BF16)
+            t_send[k] = (acc[k] + s_recv[k]).astype(BF16)
             tree_copy(k).start()
         else:
-            acc[k] = acc[k] + s_recv[k].astype(F32)
+            acc[k] = acc[k] + s_recv[k]
 
     def summed(k, j, s, w):
         out = acc[k, j, :, s : s + w]
@@ -280,9 +300,12 @@
 
     pending = [0]
     for k in arrival:
+        while k == arrival[-1] and pending:
+            j = pending.pop(0)
+            lower(j, j == 0)
         hid_tree(k).wait_recv()
         forward(k, hid_tree, hid_core)
-        if len(pending) > 2 or k == arrival[0]:
+        if len(pending) > 1:
             j = pending.pop(0)
             lower(j, j == 0)
         pending.append(k)
@@ -313,11 +336,13 @@
             hid_tree(k).wait_send()
 
 
-def layer(att, residual, norm_gain, out_weight, gate_weight, up_weight, down_weight, n_req, d_model):
+def layer(query, keys, values, lengths, residual, norm_gain, out_weight, gate_weight, up_weight, down_weight, n_req, d_model):
     rows, width = residual.shape
-    per, k_part = att.shape
+    local_reqs, local_kv, _, head_dim = keys.shape
+    group = query.shape[1] // local_kv
     k_local = out_weight.shape[0]
-    quarters = k_local // k_part
+    quarters = local_kv
+    per, k_part = quarters * local_reqs, k_local // quarters
     ff = gate_weight.shape[1]
     chunk = ff // n_req
     half = rows // 2
@@ -328,6 +353,7 @@
     vmem = lambda shape, dtype: pltpu.VMEM(shape, dtype)
     piece = (n_req, 2, half, chunk)
     scratch = [
+        vmem((per, group, head_dim), F32),
         vmem((max(in_ow * chunk, k_local), width), BF16),
         vmem((max(n_req - in_ow, 1), chunk, width), BF16),
         vmem((gu_slots, 2, width, chunk), BF16),
@@ -340,8 +366,8 @@
         vmem((bits + 2, rows, 128), F32),
         vmem((bits + 1, rows, 128), F32),
         vmem(piece, F32),
-        vmem(piece, BF16),
-        vmem(piece, BF16),
+        vmem(piece, F32),
+        vmem(piece, F32),
         vmem(piece, BF16),
         vmem(piece, BF16),
         vmem(piece, BF16),
@@ -360,16 +386,19 @@
     return pl.pallas_call(
         functools.partial(layer_kernel, n_req, quarters, d_model),
         out_shape=jax.ShapeDtypeStruct((half, width), BF16),
-        in_specs=[in_vmem] * 3 + [anywhere] * 4,
+        in_specs=[pl.BlockSpec(memory_space=pltpu.SMEM)] + [in_vmem] * 5 + [anywhere] * 4,
         out_specs=in_vmem,
         scratch_shapes=scratch,
         compiler_params=pltpu.CompilerParams(
-            collective_id=0, has_side_effects=True, vmem_limit_bytes=60 * 1024 * 1024
+            collective_id=0, has_side_effects=True, vmem_limit_bytes=62 * 1024 * 1024
         ),
         cost_estimate=pl.CostEstimate(
             flops=2 * rows * weights, bytes_accessed=2 * weights, transcendentals=0
         ),
-    )(att, residual, norm_gain.reshape(1, width), out_weight, gate_weight, up_weight, down_weight)
+    )(
+        lengths, query, keys, values, residual, norm_gain.reshape(1, width),
+        out_weight, gate_weight, up_weight, down_weight,
+    )
 
 
 def attention(query, keys, values, lengths):
@@ -424,12 +453,10 @@
 def fused_shards(
     n_req, d_model, query, keys, values, lengths, residual, out_weight, norm_gain, gate_weight, up_weight, down_weight
 ):
-    attended = attention(query, keys, values, lengths)
-    local_reqs, k_local = attended.shape
-    quarters = 16 // local_reqs
-    block = attended.reshape(local_reqs, quarters, k_local // quarters)
-    block = block.transpose(1, 0, 2).reshape(16, k_local // quarters)
-    return layer(block, residual, norm_gain, out_weight, gate_weight, up_weight, down_weight, n_req, d_model)
+    return layer(
+        query, keys, values, lengths, residual, norm_gain,
+        out_weight, gate_weight, up_weight, down_weight, n_req, d_model,
+    )
 
 
 def solution(mesh):
@@ -447,8 +474,8 @@
             and n_req & (n_req - 1) == 0
             and ff % (n_req * 128) == 0
             and rows % 32 == 0
-            and 16 % local_reqs == 0
-            and out_weight.shape[0] % ((16 // local_reqs) * 128) == 0
+            and local_reqs * keys.shape[1] == 16
+            and query.shape[2] % 128 == 0
         )
         body = functools.partial(fused_shards, n_req, d_model) if fits else functools.partial(plain_shards, d_model)
         return body(query, keys, values, lengths, residual, out_weight, norm_gain, gate_weight, up_weight, down_weight)

time: 87.5 us -> 87.7 us (level)
  Pallas kernels: 80.7 us -> 86 us
  matrix products: 2.94 us -> 0 us
  local copies, waits for them, and re-layouts: 2.56 us -> 1.47 us
  other arithmetic: 1.03 us -> 0 us
    pallas_call x1, Pallas kernels: 80.7 us -> 86 us  [layer(): pl.pallas_call(functools.partial(layer_kernel, n_req, quarters, d_model),...]
    dot_general x2 -> x0, matrix products: 2.94 us -> none  [the longest x1 1.51 us: attention(): jnp.einsum('rkgp,rkpd->rkgd', weights.astype(BF16), values, preferred_ele...]
    unnamed x3 -> x1, local copies, waits for them, and re-layouts: 1.82 us -> 1.47 us
where the time goes in v2:
time: 87.7 us; the launch traced here: 87.5 us
  Pallas kernels  86 us (98%)
  local copies, waits for them, and re-layouts  1.47 us (2%)
    pallas_call x1, Pallas kernels, layer(): pl.pallas_call(functools.partial(layer_kernel, n_req, quarters, d_model),...  86 us

profile of v2, /device:TPU:0, one launch (start us, length us, event | category | flops | bytes accessed | tf_op | source)
XLA Modules:
  0.0 87.5 jit_solution(7818042627213269316)
XLA Ops:
  0.0 86.0 %shard_map.100 = bf16[32,1024]{1,0:T(8,128)(2,1)} custom-call(s32[4]{0:T(128)} %len_ref.1, bf16[4,64,128]{2,1,0:T(8,128)(2,1)} %query_ref.1, bf16[4,4,192,128]{3,2,1,0:T(8,128)(2,1)} %key_ref.1, bf16[4,4,192,128]{3,2,1,0:T(8,128)(2,1)} %value_ref.1, bf16[64,1024]{1,0:T(8,128)(2,1)} %res_ref.1, f32[1,1024]{1,0:T(1,128)} %bitcast.1, ...), custom_call_target="tpu_custom_call" | custom-call | flops 6308233216 | bytes 98566144 | tf_op jit(solution)/shard_map/pallas_call | solution.py:386
  86.0 1.5 %copy.12 = bf16[32,1024]{1,0:T(8,128)(2,1)} copy(bf16[32,1024]{1,0:T(8,128)(2,1)} %shard_map.100) | data formatting | bytes 131072
